TPU v7x, 32 devices: a whole 2x2x4 slice. The times are simulated.
32 devices in a mesh: src: 8 (over z, y), tgt: 4 (over x, core).
Axes of the slice: x: 2, y: 2, z: 4, core: 2. Of those that a mesh axis runs over, the one named last changes fastest.
Arguments:
- signals: float32 [64, 98304], P(None, ('src', 'tgt')), may hold values from -6 to 6
- leaf_maps: float32 [768, 64, 128], P(('src', 'tgt')), may hold values from -0.5 to 0.5
- root_maps: float32 [768, 128, 64], P(('src', 'tgt')), may hold values from -0.75 to 0.75
- translations: float32 [8, 8, 64, 64], replicated, may hold values from -0.375 to 0.375
- source_list: int32 [8, 24, 4], replicated, may hold values from 0 to 47, as said below
- type_list: int32 [8, 24, 4], replicated, may hold values from 0 to 7
Outputs:
- focused: float32 [64, 98304], P(None, ('src', 'tgt'))
Inputs may be any that keep to these rules, and one draw needn't show every extreme that they name: `source_list`: entries e < 2 name one of the device's own blocks (below 24); the other entries name one of the partner's blocks (at or above 24).
All inputs are finite; a program needn't handle non-finite values.
Results may differ from a plain program's by a relative error of at most 0.00011.
Values sent between devices are 32-bit elements; how exact they have to be, the bound alone decides.
A program may use at most 64 MiB of HBM per device.

v0:
```python
import jax
import jax.numpy as jnp
import numpy as np
from jax import lax
from jax.sharding import PartitionSpec as P

HIGH = lax.Precision.HIGHEST


def translate_shared(stack, level_src, level_types, level_table):
    mats = level_table[level_types]
    picked = stack[:, :, level_src, :]
    return jnp.einsum("kers,wnkes->wnkr", mats, picked, precision=HIGH)


def run_levels(spread, first, last, count, bits, offset, source_list, type_list, translations):
    for level in range(first, last):
        order = np.arange(count) ^ 1 << (level - offset) % bits
        partner = jnp.take(spread, jnp.asarray(order, dtype=jnp.int32), axis=1)
        stack = jnp.concatenate([spread, partner], axis=2)
        spread = translate_shared(stack, source_list[level], type_list[level], translations[level])
    return spread


def local(signals, leaf_maps, root_maps, translations, source_list, type_list):
    blocks = leaf_maps.shape[0]
    rank = leaf_maps.shape[1]
    width = leaf_maps.shape[2]
    waves = signals.shape[0]
    grouped = signals.reshape(waves, blocks, width)
    levels = translations.shape[0]
    half = levels // 2
    src_count = lax.axis_size("src")
    tgt_count = lax.axis_size("tgt")
    src_bits = src_count.bit_length() - 1
    tgt_bits = tgt_count.bit_length() - 1
    coef = jnp.einsum("grb,wgb->wgr", leaf_maps, grouped, precision=HIGH)
    spread = lax.all_to_all(coef, "src", split_axis=0, concat_axis=1, tiled=True)
    spread = spread.reshape(waves // src_count, src_count, blocks, rank)
    spread = run_levels(
        spread, 0, half, src_count, src_bits, 0, source_list, type_list, translations
    )
    spread = spread.reshape(waves // src_count, src_count * blocks, rank)
    spread = lax.all_to_all(
        lax.all_to_all(spread, "src", split_axis=1, concat_axis=0, tiled=True),
        "tgt",
        split_axis=0,
        concat_axis=1,
        tiled=True,
    )
    spread = spread.reshape(waves // tgt_count, tgt_count, blocks, rank)
    spread = run_levels(
        spread, half, levels, tgt_count, tgt_bits, half, source_list, type_list, translations
    )
    spread = spread.reshape(waves // tgt_count, tgt_count * blocks, rank)
    coef = lax.all_to_all(spread, "tgt", split_axis=1, concat_axis=0, tiled=True)
    focused = jnp.einsum("gbr,wgr->wgb", root_maps, coef, precision=HIGH)
    return focused.reshape(waves, blocks * width)


def solution(mesh):
    placed = (
        P(None, ("src", "tgt")),
        P(("src", "tgt"), None, None),
        P(("src", "tgt"), None, None),
        P(),
        P(),
        P(),
    )
    return jax.shard_map(
        local, mesh=mesh, in_specs=placed, out_specs=P(None, ("src", "tgt")), check_vma=False
    )
```

profile of v0, /device:TPU:0, one launch (start us, length us, event | category | flops | bytes accessed | tf_op | source)
XLA Modules:
  0.0 170.6 jit_solution(6327512268744173265)
XLA Ops:
  0.0 2.8 %convolution_bitcast_fusion.1 = f32[64,24,64]{2,0,1:T(8,128)S(1)} fusion(f32[24,64,128]{2,1,0:T(8,128)} %param.19, f32[64,3072]{1,0:T(8,128)} %param.18), kind=kOutput, calls=%fused_computation.51 | convolution fusion | flops 150994944 | bytes 1966080 | tf_op jit(solution)/shard_map/grb,wgb->wgr/dot_general | solution.py:37
  4.5 7.4 %all-to-all-start = ((f32[8,1,12288]{2,1,0:T(1,128)}), f32[8,1,12288]{2,1,0:T(1,128)S(1)}, u32[]{:S(2)}, u32[]{:S(2)}) async-start(f32[8,1,12288]{2,1,0:T(1,128)} %reshape.718), calls=%async_computation | async-start | bytes 786432 | tf_op jit(solution)/shard_map/all_to_all | solution.py:38
  15.5 2.4 %gather_fusion.1 = f32[96,64,64]{2,1,0:T(8,128)} fusion(f32[8,64,64]{2,1,0:T(8,128)S(1)} %get-tuple-element.12, s32[1024]{0:T(1024)S(1)} %pad_clamp_fusion.18), kind=kCustom, calls=%fused_computation.9 | custom fusion | bytes 3146112 | tf_op jit(solution)/shard_map/gather | solution.py:11
  17.9 2.5 %gather_fusion.3 = f32[96,64,64]{2,1,0:T(8,128)} fusion(f32[8,64,64]{2,1,0:T(8,128)S(1)} %get-tuple-element.11, s32[1024]{0:T(1024)S(1)} %pad_clamp_fusion.15), kind=kCustom, calls=%fused_computation.11 | custom fusion | bytes 3146112 | tf_op jit(solution)/shard_map/gather | solution.py:11
  20.3 2.4 %gather_fusion.5 = f32[96,64,64]{2,1,0:T(8,128)} fusion(f32[8,64,64]{2,1,0:T(8,128)S(1)} %get-tuple-element.10, s32[1024]{0:T(1024)S(1)} %pad_clamp_fusion.12), kind=kCustom, calls=%fused_computation.13 | custom fusion | bytes 3146112 | tf_op jit(solution)/shard_map/gather | solution.py:11
  22.8 2.4 %gather_fusion.7 = f32[96,64,64]{2,1,0:T(8,128)} fusion(f32[8,64,64]{2,1,0:T(8,128)S(1)} %get-tuple-element.9, s32[1024]{0:T(1024)S(1)} %pad_clamp_fusion.10), kind=kCustom, calls=%fused_computation.15 | custom fusion | bytes 3146112 | tf_op jit(solution)/shard_map/gather | solution.py:11
  25.8 2.4 %reduce = f32[8,12288]{1,0:T(8,128)} reduce(f32[8,1,12288]{2,1,0:T(1,128)S(1)} %all-to-all-done, f32[]{:T(128)} %broadcast.418), dimensions={1}, to_apply=%all_to_all.48.reduce_sub_computation | reduce | bytes 786436 | tf_op jit(solution)/shard_map/all_to_all | solution.py:38
  33.3 2.6 %gather_fusion = f32[96,8,8,64]{3,2,1,0:T(8,128)} fusion(f32[8,8,48,64]{3,1,2,0:T(8,128)S(1)} %copy.181, s32[1024]{0:T(1024)S(1)} %pad_clamp_fusion.19), kind=kCustom, calls=%fused_computation.8 | custom fusion | bytes 3146112 | tf_op jit(solution)/shard_map/gather | solution.py:12
  35.8 6.0 %convolution_bitcast_fusion.3 = f32[8,8,24,64]{3,1,0,2:T(8,128)S(1)} fusion(f32[8,8,24,4,64]{4,1,0,3,2:T(8,128)} %bitcast.291, f32[24,4,64,64,1]{3,2,4,1,0:T(8,128)} %bitcast.290), kind=kOutput, calls=%fused_computation.59 | convolution fusion | flops 301989888 | bytes 3538944 | tf_op jit(solution)/shard_map/kers,wnkes->wnkr/dot_general | solution.py:13
  45.5 2.4 %gather_fusion.2 = f32[96,8,8,64]{3,2,1,0:T(8,128)} fusion(f32[8,8,48,64]{3,1,0,2:T(8,128)S(1)} %pad_maximum_fusion.1, s32[1024]{0:T(1024)S(1)} %pad_clamp_fusion.16), kind=kCustom, calls=%fused_computation.10 | custom fusion | bytes 3146112 | tf_op jit(solution)/shard_map/gather | solution.py:12
  47.9 6.4 %fusion.18 = f32[8,8,24,64]{3,1,0,2:T(8,128)S(1)} fusion(f32[24,4,64,64,1]{3,2,1,4,0:T(8,128)} %bitcast.289, f32[24,4,8,8,64]{4,3,2,1,0:T(8,128)} %bitcast.292), kind=kOutput, calls=%fused_computation.52 | convolution fusion | flops 301989888 | bytes 3538944 | tf_op jit(solution)/shard_map/kers,wnkes->wnkr/dot_general | solution.py:13
  58.0 2.5 %gather_fusion.4 = f32[96,8,8,64]{3,2,1,0:T(8,128)} fusion(f32[8,8,48,64]{3,1,0,2:T(8,128)S(1)} %pad_maximum_fusion.2, s32[1024]{0:T(1024)S(1)} %pad_clamp_fusion.13), kind=kCustom, calls=%fused_computation.12 | custom fusion | bytes 3146112 | tf_op jit(solution)/shard_map/gather | solution.py:12
  60.4 6.0 %fusion.21 = f32[8,8,24,64]{3,1,0,2:T(8,128)S(1)} fusion(f32[24,4,64,64,1]{3,2,1,4,0:T(8,128)} %bitcast.287, f32[24,4,8,8,64]{4,3,2,1,0:T(8,128)} %bitcast.293), kind=kOutput, calls=%fused_computation.53 | convolution fusion | flops 301989888 | bytes 3538944 | tf_op jit(solution)/shard_map/kers,wnkes->wnkr/dot_general | solution.py:13
  70.1 2.4 %gather_fusion.6 = f32[96,8,8,64]{3,2,1,0:T(8,128)} fusion(f32[8,8,48,64]{3,1,0,2:T(8,128)S(1)} %pad_maximum_fusion.3, s32[1024]{0:T(1024)S(1)} %pad_clamp_fusion.11), kind=kCustom, calls=%fused_computation.14 | custom fusion | bytes 3146112 | tf_op jit(solution)/shard_map/gather | solution.py:12
  72.5 6.0 %fusion.24 = f32[8,8,24,64]{3,1,0,2:T(8,128)S(1)} fusion(f32[24,4,64,64,1]{3,2,1,4,0:T(8,128)} %bitcast.285, f32[24,4,8,8,64]{4,3,2,1,0:T(8,128)} %bitcast.294), kind=kOutput, calls=%fused_computation.54 | convolution fusion | flops 301989888 | bytes 3538944 | tf_op jit(solution)/shard_map/kers,wnkes->wnkr/dot_general | solution.py:13
  80.7 6.0 %all-to-all-start.1 = ((f32[8,1,12288]{2,1,0:T(1,128)}), f32[8,1,12288]{2,1,0:T(1,128)S(1)}, u32[]{:S(2)}, u32[]{:S(2)}) async-start(f32[8,1,12288]{2,1,0:T(1,128)} %reshape.720), calls=%async_computation.1 | async-start | bytes 786432 | tf_op jit(solution)/shard_map/all_to_all | solution.py:45
  88.0 2.4 %gather_fusion.9 = f32[96,64,64]{2,1,0:T(8,128)} fusion(f32[8,64,64]{2,1,0:T(8,128)S(1)} %get-tuple-element.6, s32[1024]{0:T(1024)S(1)} %pad_clamp_fusion.7), kind=kCustom, calls=%fused_computation.17 | custom fusion | bytes 3146112 | tf_op jit(solution)/shard_map/gather | solution.py:11
  90.4 2.5 %gather_fusion.11 = f32[96,64,64]{2,1,0:T(8,128)} fusion(f32[8,64,64]{2,1,0:T(8,128)S(1)} %get-tuple-element.8, s32[1024]{0:T(1024)S(1)} %pad_clamp_fusion.4), kind=kCustom, calls=%fused_computation.19 | custom fusion | bytes 3146112 | tf_op jit(solution)/shard_map/gather | solution.py:11
  92.9 2.4 %gather_fusion.13 = f32[96,64,64]{2,1,0:T(8,128)} fusion(f32[8,64,64]{2,1,0:T(8,128)S(1)} %get-tuple-element.14, s32[1024]{0:T(1024)S(1)} %pad_clamp_fusion.2), kind=kCustom, calls=%fused_computation.21 | custom fusion | bytes 3146112 | tf_op jit(solution)/shard_map/gather | solution.py:11
  95.3 2.4 %gather_fusion.15 = f32[96,64,64]{2,1,0:T(8,128)} fusion(f32[8,64,64]{2,1,0:T(8,128)S(1)} %get-tuple-element.13, s32[1024]{0:T(1024)S(1)} %pad_clamp_fusion), kind=kCustom, calls=%fused_computation.23 | custom fusion | bytes 3146112 | tf_op jit(solution)/shard_map/gather | solution.py:11
  101.1 3.6 %all-to-all-start.2 = ((f32[4,1,24576]{2,1,0:T(1,128)}), f32[4,1,24576]{2,1,0:T(1,128)S(1)}, u32[]{:S(2)}, u32[]{:S(2)}) async-start(f32[4,1,24576]{2,1,0:T(1,128)} %reshape.722), calls=%async_computation.2 | async-start | bytes 786432 | tf_op jit(solution)/shard_map/all_to_all | solution.py:44
  104.7 7.2 %all-to-all-done.2 = f32[4,1,24576]{2,1,0:T(1,128)S(1)} async-done(((f32[4,1,24576]{2,1,0:T(1,128)}), f32[4,1,24576]{2,1,0:T(1,128)S(1)}, u32[]{:S(2)}, u32[]{:S(2)}) %all-to-all-start.2) | async-done | bytes 393248 | tf_op jit(solution)/shard_map/all_to_all | solution.py:44
  111.9 1.7 %reduce.2 = f32[4,24576]{1,0:T(4,128)S(1)} reduce(f32[4,1,24576]{2,1,0:T(1,128)S(1)} %all-to-all-done.2, f32[]{:T(128)} %broadcast.418), dimensions={1}, to_apply=%all_to_all.55.reduce_sub_computation | reduce | bytes 786436 | tf_op jit(solution)/shard_map/all_to_all | solution.py:44
  117.0 2.4 %gather_fusion.8 = f32[96,16,4,64]{3,1,2,0:T(8,128)} fusion(f32[16,4,48,64]{3,0,2,1:T(8,128)S(1)} %pad_maximum_fusion.4, s32[1024]{0:T(1024)S(1)} %pad_clamp_fusion.8), kind=kCustom, calls=%fused_computation.16 | custom fusion | bytes 3146112 | tf_op jit(solution)/shard_map/gather | solution.py:12
  119.4 6.0 %convolution_bitcast_fusion.2 = f32[16,4,24,64]{3,0,1,2:T(8,128)S(1)} fusion(f32[16,4,24,4,64]{4,0,1,3,2:T(8,128)} %bitcast.295, f32[24,4,64,64,1]{3,2,4,1,0:T(8,128)} %bitcast.288), kind=kOutput, calls=%fused_computation.58 | convolution fusion | flops 301989888 | bytes 3538944 | tf_op jit(solution)/shard_map/kers,wnkes->wnkr/dot_general | solution.py:13
  126.7 2.4 %gather_fusion.10 = f32[96,16,4,64]{3,1,2,0:T(8,128)} fusion(f32[16,4,48,64]{3,0,1,2:T(8,128)S(1)} %pad_maximum_fusion.5, s32[1024]{0:T(1024)S(1)} %pad_clamp_fusion.5), kind=kCustom, calls=%fused_computation.18 | custom fusion | bytes 3146112 | tf_op jit(solution)/shard_map/gather | solution.py:12
  129.1 6.0 %fusion.27 = f32[16,4,24,64]{3,0,1,2:T(8,128)S(1)} fusion(f32[24,4,64,64,1]{3,2,1,4,0:T(8,128)} %bitcast.286, f32[24,4,16,4,64]{4,2,3,1,0:T(8,128)} %bitcast.296), kind=kOutput, calls=%fused_computation.55 | convolution fusion | flops 301989888 | bytes 3538944 | tf_op jit(solution)/shard_map/kers,wnkes->wnkr/dot_general | solution.py:13
  136.5 2.5 %gather_fusion.12 = f32[96,16,4,64]{3,1,2,0:T(8,128)} fusion(f32[16,4,48,64]{3,0,1,2:T(8,128)S(1)} %pad_maximum_fusion.6, s32[1024]{0:T(1024)S(1)} %pad_clamp_fusion.3), kind=kCustom, calls=%fused_computation.20 | custom fusion | bytes 3146112 | tf_op jit(solution)/shard_map/gather | solution.py:12
  139.0 6.2 %fusion.30 = f32[16,4,24,64]{3,0,1,2:T(8,128)S(1)} fusion(f32[24,4,64,64,1]{3,2,1,4,0:T(8,128)} %bitcast.284, f32[24,4,16,4,64]{4,2,3,1,0:T(8,128)} %bitcast.297), kind=kOutput, calls=%fused_computation.56 | convolution fusion | flops 301989888 | bytes 3538944 | tf_op jit(solution)/shard_map/kers,wnkes->wnkr/dot_general | solution.py:13
  146.6 2.4 %gather_fusion.14 = f32[96,16,4,64]{3,1,2,0:T(8,128)} fusion(f32[16,4,48,64]{3,0,1,2:T(8,128)S(1)} %pad_maximum_fusion.7, s32[1024]{0:T(1024)S(1)} %pad_clamp_fusion.1), kind=kCustom, calls=%fused_computation.22 | custom fusion | bytes 3146112 | tf_op jit(solution)/shard_map/gather | solution.py:12
  149.0 6.0 %fusion.33 = f32[16,4,24,64]{3,0,1,2:T(8,128)S(1)} fusion(f32[24,4,64,64,1]{3,2,1,4,0:T(8,128)} %bitcast.283, f32[24,4,16,4,64]{4,2,3,1,0:T(8,128)} %bitcast.298), kind=kOutput, calls=%fused_computation.57 | convolution fusion | flops 301989888 | bytes 3538944 | tf_op jit(solution)/shard_map/kers,wnkes->wnkr/dot_general | solution.py:13
  156.4 9.8 %all_to_all.66 = f32[4,1,24576]{2,1,0:T(1,128)S(1)} all-to-all(f32[4,1,24576]{2,1,0:T(1,128)S(1)} %reshape.724), channel_id=1, replica_groups=mesh['src'=8,'tgt'=4] {'tgt'}, dimensions={0} | all-to-all | bytes 786432 | tf_op jit(solution)/shard_map/all_to_all | solution.py:56
  (131 shorter events, 41.3 us)
Async XLA Ops:
  0.0 168.5 %copy-start = (f32[24,128,64]{1,2,0:T(8,128)S(1)}, f32[24,128,64]{1,2,0:T(8,128)}, u32[]{:S(2)}) copy-start(f32[24,128,64]{1,2,0:T(8,128)} %param.20) | copy-start | bytes 2359300
  0.0 12.0 %copy-start.10 = (s32[8]{0:T(128)S(1)}, s32[8]{0:T(128)}, u32[]{:S(2)}) copy-start(s32[8]{0:T(128)} %constant.115) | copy-start | bytes 100
  0.0 12.0 %copy-start.4 = (s32[8,24,4]{1,2,0:T(4,128)S(1)}, s32[8,24,4]{1,2,0:T(4,128)}, u32[]{:S(2)}) copy-start(s32[8,24,4]{1,2,0:T(4,128)} %param.22) | copy-start | bytes 9220
  3.3 10.4 %copy-start.5 = (s32[8,24,4]{1,2,0:T(4,128)S(1)}, s32[8,24,4]{1,2,0:T(4,128)}, u32[]{:S(2)}) copy-start(s32[8,24,4]{1,2,0:T(4,128)} %param.23) | copy-start | bytes 9220
  4.5 20.7 %all-to-all-start = ((f32[8,1,12288]{2,1,0:T(1,128)}), f32[8,1,12288]{2,1,0:T(1,128)S(1)}, u32[]{:S(2)}, u32[]{:S(2)}) async-start(f32[8,1,12288]{2,1,0:T(1,128)} %reshape.718), calls=%async_computation | async-start | bytes 786432 | tf_op jit(solution)/shard_map/all_to_all | solution.py:38
  22.8 2.4 %copy-start.9 = (s32[8]{0:T(128)S(1)}, s32[8]{0:T(128)}, u32[]{:S(2)}) copy-start(s32[8]{0:T(128)} %constant.116) | copy-start | bytes 100
  22.8 2.4 %copy-start.8 = (s32[8]{0:T(128)S(1)}, s32[8]{0:T(128)}, u32[]{:S(2)}) copy-start(s32[8]{0:T(128)} %constant.117) | copy-start | bytes 100
  41.8 0.9 copy-start.1
  54.3 0.9 copy-start.2
  66.4 0.9 copy-start.3
  80.7 17.1 %all-to-all-start.1 = ((f32[8,1,12288]{2,1,0:T(1,128)}), f32[8,1,12288]{2,1,0:T(1,128)S(1)}, u32[]{:S(2)}, u32[]{:S(2)}) async-start(f32[8,1,12288]{2,1,0:T(1,128)} %reshape.720), calls=%async_computation.1 | async-start | bytes 786432 | tf_op jit(solution)/shard_map/all_to_all | solution.py:45
  95.3 2.4 %copy-start.7 = (s32[4]{0:T(128)S(1)}, s32[4]{0:T(128)}, u32[]{:S(2)}) copy-start(s32[4]{0:T(128)} %constant.119) | copy-start | bytes 52
  95.3 2.4 %copy-start.6 = (s32[4]{0:T(128)S(1)}, s32[4]{0:T(128)}, u32[]{:S(2)}) copy-start(s32[4]{0:T(128)} %constant.120) | copy-start | bytes 52
  101.1 10.9 %all-to-all-start.2 = ((f32[4,1,24576]{2,1,0:T(1,128)}), f32[4,1,24576]{2,1,0:T(1,128)S(1)}, u32[]{:S(2)}, u32[]{:S(2)}) async-start(f32[4,1,24576]{2,1,0:T(1,128)} %reshape.722), calls=%async_computation.2 | async-start | bytes 786432 | tf_op jit(solution)/shard_map/all_to_all | solution.py:44
where the time goes:
time: 174 us; the launch traced here: 171 us
  local copies, waits for them, and re-layouts  69.1 us (40%)
  matrix products  52.1 us (30%)
  starting transfers between devices  17.1 us (10%)
  other arithmetic  14.3 us (8%)
  blocking collectives  9.84 us (6%)
  waiting for transfers between devices  7.23 us (4%)
    dot_general x8, matrix products, translate_shared(): return jnp.einsum('kers,wnkes->wnkr', mats, picked, precision=HIGH)  48.4 us
    gather x8, local copies, waits for them, and re-layouts, translate_shared(): picked = stack[:, :, level_src, :]  19.6 us
    gather x8, local copies, waits for them, and re-layouts, translate_shared(): mats = level_table[level_types]  19.4 us
    all_to_all x1, blocking collectives, local(): lax.all_to_all(spread, 'tgt', split_axis=1, concat_axis=0, tiled=True)  9.84 us
    unnamed x30, local copies, waits for them, and re-layouts  9.29 us
    gather x14, local copies, waits for them, and re-layouts, run_levels(): partner = jnp.take(spread, jnp.asarray(order, dtype=jnp.int32), axis=1)  8.38 us
    all_to_all x1, starting transfers between devices, local(): lax.all_to_all(coef, 'src', split_axis=0, concat_axis=1, tiled=True)  7.44 us
    all_to_all x1, waiting for transfers between devices, local(): lax.all_to_all(lax.all_to_all(spread, 'src', split_axis=1, concat_axis=0,...  7.19 us
  transfers between devices with their start and end apart: 3, of which 1 were waited for; matrix products, arithmetic and copies ran while one was open for 14% of the time, Pallas kernels for 0%

commit v1 on v0

--- a/solution.py
+++ b/solution.py
@@ -1,10 +1,16 @@
+import functools
+
 import jax
 import jax.numpy as jnp
 import numpy as np
 from jax import lax
+from jax.experimental import pallas as pl
+from jax.experimental.pallas import tpu as pltpu
 from jax.sharding import PartitionSpec as P
 
 HIGH = lax.Precision.HIGHEST
+MESH = pl.DeviceIdType.MESH
+NT_DIMS = (((1,), (1,)), ((), ()))
 
 
 def translate_shared(stack, level_src, level_types, level_table):
@@ -22,7 +28,7 @@
     return spread
 
 
-def local(signals, leaf_maps, root_maps, translations, source_list, type_list):
+def local_by_axis(signals, leaf_maps, root_maps, translations, source_list, type_list):
     blocks = leaf_maps.shape[0]
     rank = leaf_maps.shape[1]
     width = leaf_maps.shape[2]
@@ -58,6 +64,270 @@
     return focused.reshape(waves, blocks * width)
 
 
+def split(value):
+    high = value.astype(jnp.bfloat16)
+    low = (value - high.astype(jnp.float32)).astype(jnp.bfloat16)
+    return high, low
+
+
+def dot_nt(a, b):
+    return lax.dot_general(a, b, NT_DIMS, preferred_element_type=jnp.float32)
+
+
+def dot_nn(a, b):
+    return lax.dot_general(a, b, (((1,), (0,)), ((), ())), preferred_element_type=jnp.float32)
+
+
+def flip_rows(value, bit):
+    rows, lanes = value.shape
+    step = 1 << bit
+    if step >= 8:
+        parts = [value[at : at + step] for at in range(0, rows, step)]
+        return jnp.concatenate([parts[i ^ 1] for i in range(len(parts))], axis=0)
+    tiles = value.reshape(rows // 8, 8, lanes)
+    up = pltpu.roll(tiles, step, 1)
+    if step == 4:
+        return up.reshape(rows, lanes)
+    down = pltpu.roll(tiles, 8 - step, 1)
+    place = lax.broadcasted_iota(jnp.int32, tiles.shape, 1)
+    return jnp.where((place // step) % 2 == 1, up, down).reshape(rows, lanes)
+
+
+def flip_scalar(value, mask, bits):
+    for bit in range(bits):
+        if mask >> bit & 1:
+            step = 1 << bit
+            value = value + step - 2 * step * ((value // step) % 2)
+    return value
+
+
+def slot_masks(slot, src_bits, tgt_bits):
+    src_mask = sum((slot >> (src_bits - 1 - bit) & 1) << bit for bit in range(src_bits))
+    return src_mask, slot >> src_bits
+
+
+def fused_kernel(
+    dims, sig, leaf, root_hbm, trans_hbm, slist, tlist, out,
+    send_buf, recv_in, recv_out, held, table, weights, root_w, root, trans,
+    send_in_sem, recv_in_sem, send_out_sem, recv_out_sem, load_sem,
+):
+    n_src, n_tgt, blocks, rank, width, levels, types, degree = dims
+    count = n_src * n_tgt
+    src_bits = n_src.bit_length() - 1
+    tgt_bits = n_tgt.bit_length() - 1
+    half = levels // 2
+    s = lax.axis_index("src")
+    t = lax.axis_index("tgt")
+    me = s * n_tgt + t
+
+    load_trans = pltpu.make_async_copy(trans_hbm, trans, load_sem.at[0])
+    load_root = pltpu.make_async_copy(root_hbm, root, load_sem.at[1])
+    load_trans.start()
+    load_root.start()
+
+    peers = []
+    for slot in range(1, count):
+        src_mask, tgt_mask = slot_masks(slot, src_bits, tgt_bits)
+        peers.append((slot, flip_scalar(s, src_mask, src_bits), flip_scalar(t, tgt_mask, tgt_bits)))
+    barrier = pltpu.get_barrier_semaphore()
+    for slot, ps, pt in peers:
+        pl.semaphore_signal(barrier, inc=1, device_id=(ps, pt), device_id_type=MESH)
+
+    def leaf_step(k, carry):
+        high, low = split(sig[:, pl.ds(pl.multiple_of(k * width, width), width)])
+        map_high, map_low = split(leaf[k])
+        y = dot_nt(high, map_high) + dot_nt(low, map_high) + dot_nt(high, map_low)
+        pair = jnp.concatenate([y[:count], y[count:]], axis=1)
+        for tile in range(count // 8):
+            send_buf[pl.ds(tile * 8 * blocks + k, 8, stride=blocks), :] = pair[tile * 8 : tile * 8 + 8]
+        return carry
+
+    lax.fori_loop(0, blocks, leaf_step, 0)
+    pl.semaphore_wait(barrier, count - 1)
+
+    copies = []
+    for slot, ps, pt in peers:
+        copies.append(
+            pltpu.make_async_remote_copy(
+                src_ref=send_buf.at[pl.ds((ps * n_tgt + pt) * blocks, blocks)],
+                dst_ref=recv_in.at[pl.ds(slot * blocks, blocks)],
+                send_sem=send_in_sem.at[slot],
+                recv_sem=recv_in_sem.at[slot],
+                device_id=(ps, pt),
+                device_id_type=MESH,
+            )
+        )
+    for copy in copies:
+        copy.start()
+    recv_in[0:blocks, :] = send_buf[pl.ds(me * blocks, blocks), :]
+
+    load_trans.wait()
+
+    def weight_step(level, carry):
+        for kind in range(types):
+            op = trans[level, kind]
+            zero = jnp.zeros_like(op)
+            pair = jnp.concatenate(
+                [jnp.concatenate([op, zero], axis=1), jnp.concatenate([zero, op], axis=1)], axis=0
+            ).T
+            high, low = split(pair)
+            lanes = pl.ds(kind * 2 * rank, 2 * rank)
+            weights[level, 0 : 2 * rank, lanes] = high
+            weights[level, 2 * rank : 4 * rank, lanes] = high
+            weights[level, 4 * rank : 6 * rank, lanes] = low
+        return carry
+
+    lax.fori_loop(0, levels, weight_step, 0)
+    load_root.wait()
+
+    def root_step(k, carry):
+        high, low = split(root[k].T)
+        root_w[k, 0:rank, :] = high
+        root_w[k, rank : 2 * rank, :] = high
+        root_w[k, 2 * rank : 3 * rank, :] = low
+        return carry
+
+    lax.fori_loop(0, blocks, root_step, 0)
+
+    for copy in copies:
+        copy.wait_recv()
+
+    def put(k, value):
+        high, low = split(value)
+        rows = pl.ds(pl.multiple_of(k * count, count), count)
+        held[rows, 0 : 2 * rank] = high
+        held[rows, 2 * rank : 4 * rank] = low
+        held[rows, 4 * rank : 6 * rank] = high
+
+    def take_step(k, carry):
+        put(
+            k,
+            jnp.concatenate(
+                [recv_in[pl.ds(tile * 8 * blocks + k, 8, stride=blocks), :] for tile in range(count // 8)],
+                axis=0,
+            ),
+        )
+        return carry
+
+    lax.fori_loop(0, blocks, take_step, 0)
+    for copy in copies:
+        copy.wait_send()
+
+    group = 256 // count
+    for level in range(levels):
+        if level < half:
+            bit = src_bits - 1 - level % src_bits
+        else:
+            bit = src_bits + (level - half) % tgt_bits
+
+        def product_step(chunk, carry, level=level):
+            rows = held[pl.ds(pl.multiple_of(chunk * group * count, group * count), group * count), :]
+            for pair in range(types // 2):
+                z = dot_nn(rows, weights[level, :, pair * 4 * rank : (pair + 1) * 4 * rank])
+                for side in range(2):
+                    table[2 * pair + side, pl.ds(chunk * group, group)] = z[
+                        :, side * 2 * rank : (side + 1) * 2 * rank
+                    ].reshape(group, count, 2 * rank)
+            return carry
+
+        lax.fori_loop(0, blocks // group, product_step, 0)
+
+        def sum_step(quad, carry, level=level, bit=bit):
+            for sub in range(4):
+                k = quad * 4 + sub
+                own = table[tlist[level, k, 0], slist[level, k, 0]]
+                for e in range(1, degree // 2):
+                    own = own + table[tlist[level, k, e], slist[level, k, e]]
+                other = table[tlist[level, k, degree // 2], jnp.maximum(slist[level, k, degree // 2] - blocks, 0)]
+                for e in range(degree // 2 + 1, degree):
+                    other = other + table[tlist[level, k, e], jnp.maximum(slist[level, k, e] - blocks, 0)]
+                total = own + flip_rows(other, bit)
+                if level < levels - 1:
+                    put(k, total)
+                else:
+                    for tile in range(count // 8):
+                        send_buf[pl.ds(tile * 8 * blocks + k, 8, stride=blocks), :] = total[
+                            tile * 8 : tile * 8 + 8
+                        ]
+            return carry
+
+        lax.fori_loop(0, blocks // 4, sum_step, 0)
+
+    returns = []
+    for slot, ps, pt in peers:
+        returns.append(
+            pltpu.make_async_remote_copy(
+                src_ref=send_buf.at[pl.ds(slot * blocks, blocks)],
+                dst_ref=recv_out.at[pl.ds(me * blocks, blocks)],
+                send_sem=send_out_sem.at[slot],
+                recv_sem=recv_out_sem.at[slot],
+                device_id=(ps, pt),
+                device_id_type=MESH,
+            )
+        )
+    for copy in returns:
+        copy.start()
+    recv_out[pl.ds(me * blocks, blocks), :] = send_buf[0:blocks, :]
+    for copy in returns:
+        copy.wait_recv()
+
+    def focus_step(k, carry):
+        pair = jnp.concatenate(
+            [recv_out[pl.ds(tile * 8 * blocks + k, 8, stride=blocks), :] for tile in range(count // 8)],
+            axis=0,
+        )
+        high, low = split(jnp.concatenate([pair[:, :rank], pair[:, rank:]], axis=0))
+        y = dot_nn(jnp.concatenate([high, low, high], axis=1), root_w[k])
+        out[:, pl.ds(pl.multiple_of(k * width, width), width)] = y
+        return carry
+
+    lax.fori_loop(0, blocks, focus_step, 0)
+    for copy in returns:
+        copy.wait_send()
+
+
+def local_fused(n_src, n_tgt, signals, leaf_maps, root_maps, translations, source_list, type_list):
+    blocks, rank, width = leaf_maps.shape
+    levels, types = translations.shape[:2]
+    degree = source_list.shape[2]
+    count = n_src * n_tgt
+    dims = (n_src, n_tgt, blocks, rank, width, levels, types, degree)
+    vmem = pl.BlockSpec(memory_space=pltpu.VMEM)
+    smem = pl.BlockSpec(memory_space=pltpu.SMEM)
+    hbm = pl.BlockSpec(memory_space=pl.ANY)
+    lanes = 2 * rank
+    return pl.pallas_call(
+        functools.partial(fused_kernel, dims),
+        out_shape=jax.ShapeDtypeStruct(signals.shape, jnp.float32),
+        in_specs=[vmem, vmem, hbm, hbm, smem, smem],
+        out_specs=vmem,
+        scratch_shapes=[
+            pltpu.VMEM((count * blocks, lanes), jnp.float32),
+            pltpu.VMEM((count * blocks, lanes), jnp.float32),
+            pltpu.VMEM((count * blocks, lanes), jnp.float32),
+            pltpu.VMEM((blocks * count, 3 * lanes), jnp.bfloat16),
+            pltpu.VMEM((types, blocks, count, lanes), jnp.float32),
+            pltpu.VMEM((levels, 3 * lanes, types * lanes), jnp.bfloat16),
+            pltpu.VMEM((blocks, 3 * rank, width), jnp.bfloat16),
+            pltpu.VMEM(root_maps.shape, jnp.float32),
+            pltpu.VMEM(translations.shape, jnp.float32),
+            pltpu.SemaphoreType.DMA((count,)),
+            pltpu.SemaphoreType.DMA((count,)),
+            pltpu.SemaphoreType.DMA((count,)),
+            pltpu.SemaphoreType.DMA((count,)),
+            pltpu.SemaphoreType.DMA((2,)),
+        ],
+        compiler_params=pltpu.CompilerParams(
+            collective_id=0, has_side_effects=True, vmem_limit_bytes=40 * 1024 * 1024
+        ),
+        cost_estimate=pl.CostEstimate(flops=10**9, bytes_accessed=5 * 10**6, transcendentals=0),
+    )(signals, leaf_maps, root_maps, translations, source_list, type_list)
+
+
+def is_power(value):
+    return value > 1 and value & (value - 1) == 0
+
+
 def solution(mesh):
     placed = (
         P(None, ("src", "tgt")),
@@ -67,6 +337,24 @@
         P(),
         P(),
     )
+    n_src, n_tgt = mesh.shape["src"], mesh.shape["tgt"]
+
+    def local(signals, leaf_maps, *rest):
+        blocks, rank, width = leaf_maps.shape
+        fits = (
+            signals.shape[0] == 2 * n_src * n_tgt
+            and is_power(n_src)
+            and is_power(n_tgt)
+            and 256 % (n_src * n_tgt) == 0
+            and blocks % 8 == 0
+            and blocks % (256 // (n_src * n_tgt)) == 0
+            and rank == 64
+            and width == 128
+        )
+        if fits:
+            return local_fused(n_src, n_tgt, signals, leaf_maps, *rest)
+        return local_by_axis(signals, leaf_maps, *rest)
+
     return jax.shard_map(
         local, mesh=mesh, in_specs=placed, out_specs=P(None, ("src", "tgt")), check_vma=False
     )

time: 174 us -> 60.3 us (0.35); the launches traced: 171 us -> 60 us
  local copies, waits for them, and re-layouts: 69.1 us -> 5.87 us
  Pallas kernels: 0 us -> 54.1 us
  matrix products: 52.1 us -> 0 us
  starting transfers between devices: 17.1 us -> 0 us
  other arithmetic: 14.3 us -> 0 us
  blocking collectives: 9.84 us -> 0 us
  waiting for transfers between devices: 7.23 us -> 0 us
    pallas_call x0 -> x1, Pallas kernels: none -> 54.1 us  [local_fused(): pl.pallas_call(functools.partial(fused_kernel, dims), out_shape=jax.Shape...]
    dot_general x10 -> x0, matrix products: 52.1 us -> none  [the longest x8 48.4 us: translate_shared(): return jnp.einsum('kers,wnkes->wnkr', mats, picked, precision=HIGH)]
    gather x30 -> x0, local copies, waits for them, and re-layouts: 47.3 us -> none  [the longest x8 19.6 us: translate_shared(): picked = stack[:, :, level_src, :]]
    all_to_all x3 -> x0, starting transfers between devices: 17.1 us -> none  [the longest x1 7.44 us: local(): lax.all_to_all(coef, 'src', split_axis=0, concat_axis=1, tiled=True)]
    all_to_all x1 -> x0, blocking collectives: 9.84 us -> none  [local(): lax.all_to_all(spread, 'tgt', split_axis=1, concat_axis=0, tiled=True)]
    all_to_all x4 -> x0, other arithmetic: 7.45 us -> none  [the longest x1 2.41 us: local(): lax.all_to_all(coef, 'src', split_axis=0, concat_axis=1, tiled=True)]
    all_to_all x3 -> x0, waiting for transfers between devices: 7.23 us -> none  [the longest x1 7.19 us: local(): lax.all_to_all(lax.all_to_all(spread, 'src', split_axis=1, concat_axis=0,...]
    concatenate x8 -> x0, other arithmetic: 6.7 us -> none  [run_levels(): stack = jnp.concatenate([spread, partner], axis=2)]
  transfers between devices with their start and end apart: 3 -> 0, of which waited for: 1 -> 0; matrix products, arithmetic and copies ran while one was open for 14% -> 0% of each run, Pallas kernels for 0% -> 0%
where the time goes in v1:
time: 60.3 us; the launch traced here: 60 us
  Pallas kernels  54.1 us (90%)
  local copies, waits for them, and re-layouts  5.87 us (10%)
    pallas_call x1, Pallas kernels, local_fused(): pl.pallas_call(functools.partial(fused_kernel, dims), out_shape=jax.Shape...  54.1 us
    unnamed x10, local copies, waits for them, and re-layouts  5.87 us

profile of v1, /device:TPU:0, one launch (start us, length us, event | category | flops | bytes accessed | tf_op | source)
XLA Modules:
  0.0 60.0 jit_solution(4458717272422149300)
XLA Ops:
  0.0 0.0 copy-start.2
  0.0 0.0 copy-start.1
  0.0 1.0 %copy.8.slist = s32[8,24,4]{2,1,0:T(8,128)S(1)} copy(s32[8,24,4]{1,2,0:T(4,128)} %param.10) | data formatting | bytes 6144 | tf_op args[4]
  1.0 0.8 %copy.9.tlist = s32[8,24,4]{2,1,0:T(8,128)S(1)} copy(s32[8,24,4]{1,2,0:T(4,128)} %param.11) | data formatting | bytes 6144 | tf_op args[5]
  1.8 1.6 %copy.7.root_hbm = f32[24,128,64]{2,1,0:T(8,128)S(1)} copy(f32[24,128,64]{1,2,0:T(8,128)} %param.8) | data formatting | bytes 1572864 | tf_op args[2]
  3.4 0.0 copy-done.2
  3.4 0.0 copy-done.1
  3.4 0.0 copy-start
  3.4 1.6 %copy-done = f32[8,8,64,64]{3,2,1,0:T(8,128)S(1)} copy-done((f32[8,8,64,64]{3,2,1,0:T(8,128)S(1)}, f32[8,8,64,64]{3,2,1,0:T(8,128)}, u32[]{:S(2)}) %copy-start) | copy-done | bytes 1048600
  5.0 54.1 %shard_map.64 = f32[64,3072]{1,0:T(8,128)S(1)} custom-call(f32[64,3072]{1,0:T(8,128)S(1)} %copy-done.1, f32[24,64,128]{2,1,0:T(8,128)S(1)} %copy-done.2, f32[24,128,64]{2,1,0:T(8,128)S(1)} %copy.7.root_hbm, f32[8,8,64,64]{3,2,1,0:T(8,128)S(1)} %copy-done, s32[8,24,4]{2,1,0:T(8,128)S(1)} %copy.8.slist, s32[8,24,4]{2,1,0:T(8,128)S(1)} %copy.9.tlist), custom_call_target="tpu_custom_call" | custom-call | flops 1000000000 | bytes 5000000 | tf_op jit(solution)/shard_map/pallas_call | solution.py:299
  59.1 0.9 %copy.11 = f32[64,3072]{1,0:T(8,128)} copy(f32[64,3072]{1,0:T(8,128)S(1)} %shard_map.64) | data formatting | bytes 1572864
Async XLA Ops:
  0.0 3.4 %copy-start.2 = (f32[24,64,128]{2,1,0:T(8,128)S(1)}, f32[24,64,128]{2,1,0:T(8,128)}, u32[]{:S(2)}) copy-start(f32[24,64,128]{2,1,0:T(8,128)} %leaf.1) | copy-start | bytes 2359300
  0.0 3.4 %copy-start.1 = (f32[64,3072]{1,0:T(8,128)S(1)}, f32[64,3072]{1,0:T(8,128)}, u32[]{:S(2)}) copy-start(f32[64,3072]{1,0:T(8,128)} %sig.1) | copy-start | bytes 2359300
  3.4 1.6 %copy-start = (f32[8,8,64,64]{3,2,1,0:T(8,128)S(1)}, f32[8,8,64,64]{3,2,1,0:T(8,128)}, u32[]{:S(2)}) copy-start(f32[8,8,64,64]{3,2,1,0:T(8,128)} %trans_hbm.1) | copy-start | bytes 3145732

commit v2 on v1

--- a/solution.py
+++ b/solution.py
@@ -107,8 +107,8 @@
 
 
 def fused_kernel(
-    dims, sig, leaf, root_hbm, trans_hbm, slist, tlist, out,
-    send_buf, recv_in, recv_out, held, table, weights, root_w, root, trans,
+    dims, sig_hbm, leaf_hbm, root_hbm, trans_hbm, slist, tlist, out,
+    send_buf, recv_in, recv_out, held, table_a, table_b, weights, root_w, sig, leaf, root, trans,
     send_in_sem, recv_in_sem, send_out_sem, recv_out_sem, load_sem,
 ):
     n_src, n_tgt, blocks, rank, width, levels, types, degree = dims
@@ -116,14 +116,21 @@
     src_bits = n_src.bit_length() - 1
     tgt_bits = n_tgt.bit_length() - 1
     half = levels // 2
+    group = 256 // count
+    chunks = blocks // group
+    tables = (table_a, table_b)
     s = lax.axis_index("src")
     t = lax.axis_index("tgt")
     me = s * n_tgt + t
 
-    load_trans = pltpu.make_async_copy(trans_hbm, trans, load_sem.at[0])
-    load_root = pltpu.make_async_copy(root_hbm, root, load_sem.at[1])
-    load_trans.start()
-    load_root.start()
+    loads = [
+        pltpu.make_async_copy(source, target, load_sem.at[i])
+        for i, (source, target) in enumerate(
+            ((sig_hbm, sig), (leaf_hbm, leaf), (trans_hbm, trans), (root_hbm, root))
+        )
+    ]
+    for load in loads:
+        load.start()
 
     peers = []
     for slot in range(1, count):
@@ -133,35 +140,46 @@
     for slot, ps, pt in peers:
         pl.semaphore_signal(barrier, inc=1, device_id=(ps, pt), device_id_type=MESH)
 
-    def leaf_step(k, carry):
-        high, low = split(sig[:, pl.ds(pl.multiple_of(k * width, width), width)])
-        map_high, map_low = split(leaf[k])
-        y = dot_nt(high, map_high) + dot_nt(low, map_high) + dot_nt(high, map_low)
-        pair = jnp.concatenate([y[:count], y[count:]], axis=1)
+    def spread_rows(ref, k, value):
         for tile in range(count // 8):
-            send_buf[pl.ds(tile * 8 * blocks + k, 8, stride=blocks), :] = pair[tile * 8 : tile * 8 + 8]
-        return carry
-
-    lax.fori_loop(0, blocks, leaf_step, 0)
-    pl.semaphore_wait(barrier, count - 1)
-
+            ref[pl.ds(tile * 8 * blocks + k, 8, stride=blocks), :] = value[tile * 8 : tile * 8 + 8]
+
+    def gather_rows(ref, k):
+        return jnp.concatenate(
+            [ref[pl.ds(tile * 8 * blocks + k, 8, stride=blocks), :] for tile in range(count // 8)],
+            axis=0,
+        )
+
+    loads[0].wait()
+    loads[1].wait()
     copies = []
-    for slot, ps, pt in peers:
-        copies.append(
-            pltpu.make_async_remote_copy(
-                src_ref=send_buf.at[pl.ds((ps * n_tgt + pt) * blocks, blocks)],
-                dst_ref=recv_in.at[pl.ds(slot * blocks, blocks)],
-                send_sem=send_in_sem.at[slot],
-                recv_sem=recv_in_sem.at[slot],
+    for chunk in range(chunks):
+        for k in range(chunk * group, (chunk + 1) * group):
+            high, low = split(sig[:, k * width : (k + 1) * width])
+            map_high, map_low = split(leaf[k])
+            y = dot_nt(
+                jnp.concatenate([high, low, high], axis=1),
+                jnp.concatenate([map_high, map_high, map_low], axis=1),
+            )
+            spread_rows(send_buf, k, jnp.concatenate([y[:count], y[count:]], axis=1))
+        if chunk == 0:
+            pl.semaphore_wait(barrier, count - 1)
+        started = []
+        for slot, ps, pt in reversed(peers):
+            copy = pltpu.make_async_remote_copy(
+                src_ref=send_buf.at[pl.ds((ps * n_tgt + pt) * blocks + chunk * group, group)],
+                dst_ref=recv_in.at[pl.ds(slot * blocks + chunk * group, group)],
+                send_sem=send_in_sem.at[chunk, slot],
+                recv_sem=recv_in_sem.at[chunk, slot],
                 device_id=(ps, pt),
                 device_id_type=MESH,
             )
-        )
-    for copy in copies:
-        copy.start()
+            copy.start()
+            started.append(copy)
+        copies.append(started)
     recv_in[0:blocks, :] = send_buf[pl.ds(me * blocks, blocks), :]
 
-    load_trans.wait()
+    loads[2].wait()
 
     def weight_step(level, carry):
         for kind in range(types):
@@ -178,10 +196,10 @@
         return carry
 
     lax.fori_loop(0, levels, weight_step, 0)
-    load_root.wait()
+    loads[3].wait()
 
     def root_step(k, carry):
-        high, low = split(root[k].T)
+        high, low = split(root[k])
         root_w[k, 0:rank, :] = high
         root_w[k, rank : 2 * rank, :] = high
         root_w[k, 2 * rank : 3 * rank, :] = low
@@ -189,101 +207,85 @@
 
     lax.fori_loop(0, blocks, root_step, 0)
 
-    for copy in copies:
-        copy.wait_recv()
-
     def put(k, value):
         high, low = split(value)
-        rows = pl.ds(pl.multiple_of(k * count, count), count)
+        rows = slice(k * count, (k + 1) * count)
         held[rows, 0 : 2 * rank] = high
         held[rows, 2 * rank : 4 * rank] = low
         held[rows, 4 * rank : 6 * rank] = high
 
-    def take_step(k, carry):
-        put(
-            k,
-            jnp.concatenate(
-                [recv_in[pl.ds(tile * 8 * blocks + k, 8, stride=blocks), :] for tile in range(count // 8)],
-                axis=0,
-            ),
-        )
-        return carry
-
-    lax.fori_loop(0, blocks, take_step, 0)
-    for copy in copies:
-        copy.wait_send()
-
-    group = 256 // count
-    for level in range(levels):
+    def multiply(level, chunk):
+        rows = held[chunk * group * count : (chunk + 1) * group * count, :]
+        for pair in range(types // 2):
+            z = dot_nn(rows, weights[level, :, pair * 4 * rank : (pair + 1) * 4 * rank])
+            for side in range(2):
+                tables[level % 2][2 * pair + side, chunk * group : (chunk + 1) * group] = z[
+                    :, side * 2 * rank : (side + 1) * 2 * rank
+                ].reshape(group, count, 2 * rank)
+
+    def add_up(level, k):
         if level < half:
             bit = src_bits - 1 - level % src_bits
         else:
             bit = src_bits + (level - half) % tgt_bits
-
-        def product_step(chunk, carry, level=level):
-            rows = held[pl.ds(pl.multiple_of(chunk * group * count, group * count), group * count), :]
-            for pair in range(types // 2):
-                z = dot_nn(rows, weights[level, :, pair * 4 * rank : (pair + 1) * 4 * rank])
-                for side in range(2):
-                    table[2 * pair + side, pl.ds(chunk * group, group)] = z[
-                        :, side * 2 * rank : (side + 1) * 2 * rank
-                    ].reshape(group, count, 2 * rank)
-            return carry
-
-        lax.fori_loop(0, blocks // group, product_step, 0)
-
-        def sum_step(quad, carry, level=level, bit=bit):
-            for sub in range(4):
-                k = quad * 4 + sub
-                own = table[tlist[level, k, 0], slist[level, k, 0]]
-                for e in range(1, degree // 2):
-                    own = own + table[tlist[level, k, e], slist[level, k, e]]
-                other = table[tlist[level, k, degree // 2], jnp.maximum(slist[level, k, degree // 2] - blocks, 0)]
-                for e in range(degree // 2 + 1, degree):
-                    other = other + table[tlist[level, k, e], jnp.maximum(slist[level, k, e] - blocks, 0)]
-                total = own + flip_rows(other, bit)
-                if level < levels - 1:
-                    put(k, total)
-                else:
-                    for tile in range(count // 8):
-                        send_buf[pl.ds(tile * 8 * blocks + k, 8, stride=blocks), :] = total[
-                            tile * 8 : tile * 8 + 8
-                        ]
-            return carry
-
-        lax.fori_loop(0, blocks // 4, sum_step, 0)
+        table = tables[level % 2]
+        own = other = None
+        for e in range(degree):
+            source = slist[level, e, k]
+            if e < degree // 2:
+                part = table[tlist[level, e, k], source]
+                own = part if own is None else own + part
+            else:
+                part = table[tlist[level, e, k], jnp.maximum(source - blocks, 0)]
+                other = part if other is None else other + part
+        return own + flip_rows(other, bit)
+
+    for chunk in range(chunks):
+        for copy in copies[chunk]:
+            copy.wait_recv()
+        for k in range(chunk * group, (chunk + 1) * group):
+            put(k, gather_rows(recv_in, k))
+        multiply(0, chunk)
+    for started in copies:
+        for copy in started:
+            copy.wait_send()
+
+    for level in range(levels - 1):
+        for chunk in range(chunks):
+            for k in range(chunk * group, (chunk + 1) * group):
+                put(k, add_up(level, k))
+            multiply(level + 1, chunk)
 
     returns = []
-    for slot, ps, pt in peers:
-        returns.append(
-            pltpu.make_async_remote_copy(
-                src_ref=send_buf.at[pl.ds(slot * blocks, blocks)],
-                dst_ref=recv_out.at[pl.ds(me * blocks, blocks)],
-                send_sem=send_out_sem.at[slot],
-                recv_sem=recv_out_sem.at[slot],
+    for chunk in range(chunks):
+        for k in range(chunk * group, (chunk + 1) * group):
+            spread_rows(send_buf, k, add_up(levels - 1, k))
+        started = []
+        for slot, ps, pt in reversed(peers):
+            copy = pltpu.make_async_remote_copy(
+                src_ref=send_buf.at[pl.ds(slot * blocks + chunk * group, group)],
+                dst_ref=recv_out.at[pl.ds(me * blocks + chunk * group, group)],
+                send_sem=send_out_sem.at[chunk, slot],
+                recv_sem=recv_out_sem.at[chunk, slot],
                 device_id=(ps, pt),
                 device_id_type=MESH,
             )
-        )
-    for copy in returns:
-        copy.start()
+            copy.start()
+            started.append(copy)
+        returns.append(started)
     recv_out[pl.ds(me * blocks, blocks), :] = send_buf[0:blocks, :]
-    for copy in returns:
-        copy.wait_recv()
-
-    def focus_step(k, carry):
-        pair = jnp.concatenate(
-            [recv_out[pl.ds(tile * 8 * blocks + k, 8, stride=blocks), :] for tile in range(count // 8)],
-            axis=0,
-        )
-        high, low = split(jnp.concatenate([pair[:, :rank], pair[:, rank:]], axis=0))
-        y = dot_nn(jnp.concatenate([high, low, high], axis=1), root_w[k])
-        out[:, pl.ds(pl.multiple_of(k * width, width), width)] = y
-        return carry
-
-    lax.fori_loop(0, blocks, focus_step, 0)
-    for copy in returns:
-        copy.wait_send()
+
+    for chunk in range(chunks):
+        for copy in returns[chunk]:
+            copy.wait_recv()
+        for k in range(chunk * group, (chunk + 1) * group):
+            pair = gather_rows(recv_out, k)
+            high, low = split(jnp.concatenate([pair[:, :rank], pair[:, rank:]], axis=0))
+            y = dot_nn(jnp.concatenate([high, low, high], axis=1), root_w[k])
+            out[:, k * width : (k + 1) * width] = y
+    for started in returns:
+        for copy in started:
+            copy.wait_send()
 
 
 def local_fused(n_src, n_tgt, signals, leaf_maps, root_maps, translations, source_list, type_list):
@@ -296,10 +298,11 @@
     smem = pl.BlockSpec(memory_space=pltpu.SMEM)
     hbm = pl.BlockSpec(memory_space=pl.ANY)
     lanes = 2 * rank
+    chunks = blocks // (256 // count)
     return pl.pallas_call(
         functools.partial(fused_kernel, dims),
         out_shape=jax.ShapeDtypeStruct(signals.shape, jnp.float32),
-        in_specs=[vmem, vmem, hbm, hbm, smem, smem],
+        in_specs=[hbm, hbm, hbm, hbm, smem, smem],
         out_specs=vmem,
         scratch_shapes=[
             pltpu.VMEM((count * blocks, lanes), jnp.float32),
@@ -307,21 +310,31 @@
             pltpu.VMEM((count * blocks, lanes), jnp.float32),
             pltpu.VMEM((blocks * count, 3 * lanes), jnp.bfloat16),
             pltpu.VMEM((types, blocks, count, lanes), jnp.float32),
+            pltpu.VMEM((types, blocks, count, lanes), jnp.float32),
             pltpu.VMEM((levels, 3 * lanes, types * lanes), jnp.bfloat16),
             pltpu.VMEM((blocks, 3 * rank, width), jnp.bfloat16),
-            pltpu.VMEM(root_maps.shape, jnp.float32),
+            pltpu.VMEM(signals.shape, jnp.float32),
+            pltpu.VMEM(leaf_maps.shape, jnp.float32),
+            pltpu.VMEM((blocks, rank, width), jnp.float32),
             pltpu.VMEM(translations.shape, jnp.float32),
-            pltpu.SemaphoreType.DMA((count,)),
-            pltpu.SemaphoreType.DMA((count,)),
-            pltpu.SemaphoreType.DMA((count,)),
-            pltpu.SemaphoreType.DMA((count,)),
-            pltpu.SemaphoreType.DMA((2,)),
+            pltpu.SemaphoreType.DMA((chunks, count)),
+            pltpu.SemaphoreType.DMA((chunks, count)),
+            pltpu.SemaphoreType.DMA((chunks, count)),
+            pltpu.SemaphoreType.DMA((chunks, count)),
+            pltpu.SemaphoreType.DMA((4,)),
         ],
         compiler_params=pltpu.CompilerParams(
-            collective_id=0, has_side_effects=True, vmem_limit_bytes=40 * 1024 * 1024
+            collective_id=0, has_side_effects=True, vmem_limit_bytes=58 * 1024 * 1024
         ),
         cost_estimate=pl.CostEstimate(flops=10**9, bytes_accessed=5 * 10**6, transcendentals=0),
-    )(signals, leaf_maps, root_maps, translations, source_list, type_list)
+    )(
+        signals,
+        leaf_maps,
+        jnp.swapaxes(root_maps, 1, 2),
+        translations,
+        jnp.swapaxes(source_list, 1, 2),
+        jnp.swapaxes(type_list, 1, 2),
+    )
 
 
 def is_power(value):

time: 60.3 us -> 44.6 us (0.74)
  Pallas kernels: 54.1 us -> 42.2 us
  local copies, waits for them, and re-layouts: 5.87 us -> 2.07 us
    pallas_call x1, Pallas kernels: 54.1 us -> 42.2 us  [local_fused(): pl.pallas_call(functools.partial(fused_kernel, dims), out_shape=jax.Shape...]
    unnamed x10 -> x1, local copies, waits for them, and re-layouts: 5.87 us -> 2.07 us
where the time goes in v2:
time: 44.6 us; the launch traced here: 44.3 us
  Pallas kernels  42.2 us (95%)
  local copies, waits for them, and re-layouts  2.07 us (5%)
    pallas_call x1, Pallas kernels, local_fused(): pl.pallas_call(functools.partial(fused_kernel, dims), out_shape=jax.Shape...  42.2 us
    unnamed x1, local copies, waits for them, and re-layouts  2.07 us

profile of v2, /device:TPU:0, one launch (start us, length us, event | category | flops | bytes accessed | tf_op | source)
XLA Modules:
  0.0 44.3 jit_solution(9490389465091343278)
XLA Ops:
  0.0 42.2 %shard_map.64 = f32[64,3072]{1,0:T(8,128)} custom-call(f32[64,3072]{1,0:T(8,128)} %sig_hbm.1, f32[24,64,128]{2,1,0:T(8,128)} %leaf_hbm.1, f32[24,64,128]{2,1,0:T(8,128)} %bitcast.3, f32[8,8,64,64]{3,2,1,0:T(8,128)} %trans_hbm.1, s32[8,4,24]{2,1,0:T(4,128)} %bitcast.4, s32[8,4,24]{2,1,0:T(4,128)} %bitcast.5), custom_call_target="tpu_custom_call" | custom-call | flops 1000000000 | bytes 5000000 | tf_op jit(solution)/shard_map/pallas_call | solution.py:302
  42.2 2.1 %copy.8 = f32[64,3072]{1,0:T(8,128)} copy(f32[64,3072]{1,0:T(8,128)} %shard_map.64) | data formatting | bytes 1572864

commit v3 on v2

--- a/solution.py
+++ b/solution.py
@@ -150,9 +150,12 @@
             axis=0,
         )
 
+    def wait_bytes(ref, rows, sem):
+        part = ref.at[pl.ds(0, rows)]
+        pltpu.make_async_copy(part, part, sem).wait()
+
     loads[0].wait()
     loads[1].wait()
-    copies = []
     for chunk in range(chunks):
         for k in range(chunk * group, (chunk + 1) * group):
             high, low = split(sig[:, k * width : (k + 1) * width])
@@ -164,19 +167,16 @@
             spread_rows(send_buf, k, jnp.concatenate([y[:count], y[count:]], axis=1))
         if chunk == 0:
             pl.semaphore_wait(barrier, count - 1)
-        started = []
         for slot, ps, pt in reversed(peers):
             copy = pltpu.make_async_remote_copy(
                 src_ref=send_buf.at[pl.ds((ps * n_tgt + pt) * blocks + chunk * group, group)],
                 dst_ref=recv_in.at[pl.ds(slot * blocks + chunk * group, group)],
-                send_sem=send_in_sem.at[chunk, slot],
-                recv_sem=recv_in_sem.at[chunk, slot],
+                send_sem=send_in_sem.at[0],
+                recv_sem=recv_in_sem.at[chunk],
                 device_id=(ps, pt),
                 device_id_type=MESH,
             )
             copy.start()
-            started.append(copy)
-        copies.append(started)
     recv_in[0:blocks, :] = send_buf[pl.ds(me * blocks, blocks), :]
 
     loads[2].wait()
@@ -241,14 +241,11 @@
         return own + flip_rows(other, bit)
 
     for chunk in range(chunks):
-        for copy in copies[chunk]:
-            copy.wait_recv()
+        wait_bytes(recv_in, (count - 1) * group, recv_in_sem.at[chunk])
         for k in range(chunk * group, (chunk + 1) * group):
             put(k, gather_rows(recv_in, k))
         multiply(0, chunk)
-    for started in copies:
-        for copy in started:
-            copy.wait_send()
+    wait_bytes(send_buf, (count - 1) * blocks, send_in_sem.at[0])
 
     for level in range(levels - 1):
         for chunk in range(chunks):
@@ -256,36 +253,29 @@
                 put(k, add_up(level, k))
             multiply(level + 1, chunk)
 
-    returns = []
     for chunk in range(chunks):
         for k in range(chunk * group, (chunk + 1) * group):
             spread_rows(send_buf, k, add_up(levels - 1, k))
-        started = []
         for slot, ps, pt in reversed(peers):
             copy = pltpu.make_async_remote_copy(
                 src_ref=send_buf.at[pl.ds(slot * blocks + chunk * group, group)],
                 dst_ref=recv_out.at[pl.ds(me * blocks + chunk * group, group)],
-                send_sem=send_out_sem.at[chunk, slot],
-                recv_sem=recv_out_sem.at[chunk, slot],
+                send_sem=send_out_sem.at[0],
+                recv_sem=recv_out_sem.at[chunk],
                 device_id=(ps, pt),
                 device_id_type=MESH,
             )
             copy.start()
-            started.append(copy)
-        returns.append(started)
     recv_out[pl.ds(me * blocks, blocks), :] = send_buf[0:blocks, :]
 
     for chunk in range(chunks):
-        for copy in returns[chunk]:
-            copy.wait_recv()
+        wait_bytes(recv_out, (count - 1) * group, recv_out_sem.at[chunk])
         for k in range(chunk * group, (chunk + 1) * group):
             pair = gather_rows(recv_out, k)
             high, low = split(jnp.concatenate([pair[:, :rank], pair[:, rank:]], axis=0))
             y = dot_nn(jnp.concatenate([high, low, high], axis=1), root_w[k])
             out[:, k * width : (k + 1) * width] = y
-    for started in returns:
-        for copy in started:
-            copy.wait_send()
+    wait_bytes(send_buf, (count - 1) * blocks, send_out_sem.at[0])
 
 
 def local_fused(n_src, n_tgt, signals, leaf_maps, root_maps, translations, source_list, type_list):
@@ -317,10 +307,10 @@
             pltpu.VMEM(leaf_maps.shape, jnp.float32),
             pltpu.VMEM((blocks, rank, width), jnp.float32),
             pltpu.VMEM(translations.shape, jnp.float32),
-            pltpu.SemaphoreType.DMA((chunks, count)),
-            pltpu.SemaphoreType.DMA((chunks, count)),
-            pltpu.SemaphoreType.DMA((chunks, count)),
-            pltpu.SemaphoreType.DMA((chunks, count)),
+            pltpu.SemaphoreType.DMA((1,)),
+            pltpu.SemaphoreType.DMA((chunks,)),
+            pltpu.SemaphoreType.DMA((1,)),
+            pltpu.SemaphoreType.DMA((chunks,)),
             pltpu.SemaphoreType.DMA((4,)),
         ],
         compiler_params=pltpu.CompilerParams(

time: 44.6 us -> 40.9 us (0.917)
  Pallas kernels: 42.2 us -> 38.5 us
    pallas_call x1, Pallas kernels: 42.2 us -> 38.5 us  [local_fused(): pl.pallas_call(functools.partial(fused_kernel, dims), out_shape=jax.Shape...]
where the time goes in v3:
time: 40.9 us; the launch traced here: 40.6 us
  Pallas kernels  38.5 us (94%)
  local copies, waits for them, and re-layouts  2.07 us (5%)
    pallas_call x1, Pallas kernels, local_fused(): pl.pallas_call(functools.partial(fused_kernel, dims), out_shape=jax.Shape...  38.5 us
    unnamed x1, local copies, waits for them, and re-layouts  2.07 us

profile of v3, /device:TPU:0, one launch (start us, length us, event | category | flops | bytes accessed | tf_op | source)
XLA Modules:
  0.0 40.6 jit_solution(5414825411204907431)
XLA Ops:
  0.0 38.5 %shard_map.64 = f32[64,3072]{1,0:T(8,128)} custom-call(f32[64,3072]{1,0:T(8,128)} %sig_hbm.1, f32[24,64,128]{2,1,0:T(8,128)} %leaf_hbm.1, f32[24,64,128]{2,1,0:T(8,128)} %bitcast.3, f32[8,8,64,64]{3,2,1,0:T(8,128)} %trans_hbm.1, s32[8,4,24]{2,1,0:T(4,128)} %bitcast.4, s32[8,4,24]{2,1,0:T(4,128)} %bitcast.5), custom_call_target="tpu_custom_call" | custom-call | flops 1000000000 | bytes 5000000 | tf_op jit(solution)/shard_map/pallas_call | solution.py:292
  38.5 2.1 %copy.8 = f32[64,3072]{1,0:T(8,128)} copy(f32[64,3072]{1,0:T(8,128)} %shard_map.64) | data formatting | bytes 1572864

commit v4 on v3

--- a/solution.py
+++ b/solution.py
@@ -184,10 +184,9 @@
     def weight_step(level, carry):
         for kind in range(types):
             op = trans[level, kind]
-            zero = jnp.zeros_like(op)
-            pair = jnp.concatenate(
-                [jnp.concatenate([op, zero], axis=1), jnp.concatenate([zero, op], axis=1)], axis=0
-            ).T
+            both = jnp.concatenate([op, op], axis=0).T
+            first = lax.broadcasted_iota(jnp.int32, both.shape, 1) < rank
+            pair = jnp.concatenate([jnp.where(first, both, 0.0), jnp.where(first, 0.0, both)], axis=0)
             high, low = split(pair)
             lanes = pl.ds(kind * 2 * rank, 2 * rank)
             weights[level, 0 : 2 * rank, lanes] = high

time: 40.9 us -> 40.9 us (level)
  no operation moved by 1% of the time
where the time goes in v4:
time: 40.9 us; the launch traced here: 40.6 us
  Pallas kernels  38.5 us (94%)
  local copies, waits for them, and re-layouts  2.07 us (5%)
    pallas_call x1, Pallas kernels, local_fused(): pl.pallas_call(functools.partial(fused_kernel, dims), out_shape=jax.Shape...  38.5 us
    unnamed x1, local copies, waits for them, and re-layouts  2.07 us

profile of v4, /device:TPU:0, one launch (start us, length us, event | category | flops | bytes accessed | tf_op | source)
XLA Modules:
  0.0 40.6 jit_solution(3847332790625418801)
XLA Ops:
  0.0 38.5 %shard_map.64 = f32[64,3072]{1,0:T(8,128)} custom-call(f32[64,3072]{1,0:T(8,128)} %sig_hbm.1, f32[24,64,128]{2,1,0:T(8,128)} %leaf_hbm.1, f32[24,64,128]{2,1,0:T(8,128)} %bitcast.3, f32[8,8,64,64]{3,2,1,0:T(8,128)} %trans_hbm.1, s32[8,4,24]{2,1,0:T(4,128)} %bitcast.4, s32[8,4,24]{2,1,0:T(4,128)} %bitcast.5), custom_call_target="tpu_custom_call" | custom-call | flops 1000000000 | bytes 5000000 | tf_op jit(solution)/shard_map/pallas_call | solution.py:291
  38.6 2.1 %copy.8 = f32[64,3072]{1,0:T(8,128)} copy(f32[64,3072]{1,0:T(8,128)} %shard_map.64) | data formatting | bytes 1572864
